TPU v7x, 128 devices: a whole 4x4x4 slice. The times are simulated.
128 devices in a mesh: section: 2 (over z_lo), dp: 16 (over x, y), tensor: 4 (over z_hi, core).
Axes of the slice: x: 4, y: 4, z: 4 (z_hi: 2, z_lo: 2; z = z_hi * 2 + z_lo), core: 2. Of those that a mesh axis runs over, the one named last changes fastest.
Arguments:
- tokens: bfloat16 [8192, 1024], P('dp'), may hold values from -6 to 6
- lengths: int32 [32, 4], P('dp'), may hold values from 1 to 170, 256 in all within a row
- cotangent: bfloat16 [8192, 1024], P('dp'), may hold values from -6 to 6
- qkv_weight: bfloat16 [2, 1024, 3, 1024], P('section', None, None, 'tensor'), may hold values from -0.1875 to 0.1875
- out_weight: bfloat16 [2, 1024, 1024], P('section', 'tensor'), may hold values from -1.5 to 1.5
- up_weight: bfloat16 [2, 1024, 4096], P('section', None, 'tensor'), may hold values from -0.1875 to 0.1875
- down_weight: bfloat16 [2, 4096, 1024], P('section', 'tensor'), may hold values from -0.09375 to 0.09375
- norm_gains: float32 [2, 2, 1024], P('section'), may hold values from 0.1 to 1.9
- feat_weights: float32 [2, 16, 64], P('section', 'tensor'), may hold values from 0.25 to 4
Outputs:
- acts: bfloat16 [2, 8192, 1024], P('section', 'dp')
- in_grads: float32 [2, 8192, 1024], P('section', 'dp')
- qkv_grad: float32 [2, 1024, 3, 1024], P('section', None, None, 'tensor')
- out_grad: float32 [2, 1024, 1024], P('section', 'tensor')
- up_grad: float32 [2, 1024, 4096], P('section', None, 'tensor')
- down_grad: float32 [2, 4096, 1024], P('section', 'tensor')
- gain_grad: float32 [2, 2, 1024], P('section')
- feat_grad: float32 [2, 16, 64], P('section', 'tensor')
Inputs may be any that keep to these rules, and one draw needn't show every extreme that they name: `lengths`: row r describes micro-batch r % 2 of index r // 2 of dp: the 4 sequences packed one after another into its 256 tokens, which they fill exactly.
All inputs are finite; a program needn't handle non-finite values.
Results may differ from a plain program's by a relative error of at most 0.033.
Values may be sent and summed in bfloat16 or wider, within the bound.
A program may use at most 192 MiB of HBM per device.

v0:
```python
import functools
import math

import jax
import jax.numpy as jnp
import numpy as np
from jax import lax
from jax.experimental import pallas as pl
from jax.experimental.pallas import tpu as pltpu
from jax.sharding import PartitionSpec as P

F32 = jnp.float32
BF16 = jnp.bfloat16
MESH = pl.DeviceIdType.MESH
EPS = 1e-05
ROWS = 256
HALF = 128
WIDTH = 1024
LOCAL = 256
HEADS = 4
DIM = 64
ROT = 16
MICROS = 2
ALL_ROWS = MICROS * ROWS


def feature_table(head_dim, feat_count):
    golden = 0.6180339887498949
    row_grid = np.arange(feat_count)[:, None] + 0.5
    columns = np.arange(head_dim)[None, :] * 1.0
    points = np.mod(row_grid * (2.0 * columns + 1.0) / feat_count + golden * columns, 1.0)
    radius = np.sqrt(-2.0 * np.log(points[:, 0::2]))
    turning = 2.0 * np.pi * points[:, 1::2]
    omega_rows = np.stack([radius * np.cos(turning), radius * np.sin(turning)], axis=2).reshape(
        feat_count, head_dim
    )
    frequency = np.arange(head_dim)[:, None] * 1.0
    cosine_basis = np.sqrt(2.0 / head_dim) * np.cos(
        np.pi * (2.0 * columns + 1.0) * frequency / (2.0 * head_dim)
    )
    cosine_basis = np.where(frequency == 0, np.sqrt(0.5), 1.0) * cosine_basis
    return np.sum(omega_rows[:, :, None] * cosine_basis[None, :, :], axis=1)


def low_pieces(values):
    high = values.astype(BF16)
    rest = (values - high.astype(values.dtype)).astype(BF16)
    return high, rest


def constants():
    table = feature_table(DIM, DIM).astype(np.float32)
    eye = np.eye(HEADS, dtype=np.float32)
    blocks = np.kron(eye, table.T / math.sqrt(DIM)).astype(np.float32)
    ones = np.kron(eye, np.ones((DIM, DIM), np.float32))
    high, rest = low_pieces(blocks)
    scaled = (ones * (-1.0 / (2.0 * DIM))).astype(BF16)
    forward = np.concatenate([high, high, rest, scaled, scaled], axis=0)
    backward = np.concatenate([blocks.T.astype(BF16), (ones / DIM).astype(BF16)], axis=1)
    half_rot = ROT // 2
    inverse = (10000.0 ** (-2.0 * np.arange(half_rot) / ROT)).astype(np.float32)
    angles = np.arange(ROWS, dtype=np.float32)[:, None] * inverse[None, :]
    cosine = np.ones((ROWS, DIM), np.float32)
    sine = np.zeros((ROWS, DIM), np.float32)
    for start in (0, half_rot):
        cosine[:, start : start + half_rot] = np.cos(angles.astype(np.float64))
        sine[:, start : start + half_rot] = np.sin(angles.astype(np.float64))
    cosine = np.tile(cosine, (1, HEADS))
    sine = np.tile(sine, (1, HEADS))
    turns = np.concatenate([*low_pieces(cosine), *low_pieces(sine)], axis=1)
    spread = np.tile(np.eye(DIM, dtype=np.float32), (1, HEADS))
    return np.concatenate(
        [
            *np.split(turns, 4, axis=1), forward, *np.split(backward, 2, axis=1), ones.astype(BF16),
            spread.astype(BF16),
        ],
        axis=0,
    )


def dot_nn(a, b):
    return lax.dot_general(a, b, (((1,), (0,)), ((), ())), preferred_element_type=F32)


def dot_nt(a, b):
    return lax.dot_general(a, b, (((1,), (1,)), ((), ())), preferred_element_type=F32)


def dot_exact(a, b, side):
    return lax.dot_general(
        a, b, (((1,), (side,)), ((), ())), preferred_element_type=F32,
        precision=lax.Precision.HIGHEST,
    )


def dot_tn(a, b):
    return lax.dot_general(a, b, (((0,), (0,)), ((), ())), preferred_element_type=F32)


def normal_cdf(v):
    bell = jnp.exp(-0.5 * v * v)
    t = pl.reciprocal(1.0 + (0.3275911 * math.sqrt(0.5)) * jnp.abs(v))
    poly = 0.5 * 1.061405429 * t - 0.5 * 1.453152027
    for coefficient in (1.421413741, -0.284496736, 0.254829592):
        poly = poly * t + 0.5 * coefficient
    tail = poly * t * bell
    cdf = jnp.where(v >= 0.0, 1.0 - tail, tail)
    return cdf, cdf + v * bell * (1.0 / math.sqrt(2.0 * math.pi))


def ln_rows(x):
    mean = jnp.mean(x, axis=-1, keepdims=True)
    centered = x - mean
    inv = lax.rsqrt(jnp.mean(centered * centered, axis=-1, keepdims=True) + EPS)
    return centered * inv, inv


def ln_back(combined, normed, inv):
    mean_c = jnp.mean(combined, axis=-1, keepdims=True)
    mean_p = jnp.mean(combined * normed, axis=-1, keepdims=True)
    return inv * (combined - mean_c - normed * mean_p)


DOWN, UP, ATTN, OUT = range(4)
ORDER = (
    (DOWN, 2), (ATTN, 1), (UP, 2), (OUT, 0), (DOWN, 3), (ATTN, 2),
    (OUT, 1), (UP, 3), (OUT, 2), (ATTN, 3), (OUT, 3), (DOWN, 4),
    (OUT, 4), (UP, 4), (OUT, 5), (ATTN, 4), (OUT, 6), (DOWN, 5),
    (UP, 5), (ATTN, 5), (DOWN, 6), (UP, 6), (ATTN, 6),
)


def wrap(v):
    return lax.rem(v + 8, 4)


class Sums:
    LAST = 6

    def __init__(self, own, g, row0, near, far, sent, got, place, at):
        self.own, self.g, self.row0, self.at = own, g, row0, at
        self.near, self.far, self.sent, self.got, self.place = near, far, sent, got, place

    def ends(self, q):
        axis1, axis2 = ("x", "y") if q == 0 else ("y", "x")
        return axis1, axis2, self.place[axis1], self.place[axis2]

    def half(self, q, b, h):
        return pl.ds(pl.multiple_of(self.row0 + q * 512 + b * 128 + h * 64, 64), 64)

    def piece(self, q, k):
        _, _, p1, _ = self.ends(q)
        return pl.ds(pl.multiple_of(self.row0 + q * 512 + p1 * 128 + k * 32, 32), 32)

    def near_piece(self, q, k):
        return (q, 2 + k // 2, pl.ds(pl.multiple_of(lax.rem(k, 2) * 32, 32), 32))

    def copies(self, q, t):
        axis1, axis2, p1, p2 = self.ends(q)
        near, own, g = self.near, self.own, self.g
        up, down = (axis1, 1), (axis1, 3)
        if t == 0:
            plan = [
                (own.at[self.half(q, wrap(p1 + 2), 0)], near.at[q, 0], up, 0),
                (own.at[self.half(q, wrap(p1 + 2), 1)], near.at[q, 1], down, 0),
                (own.at[self.half(q, wrap(p1 + 1), 1)], near.at[q, 3], up, 1),
                (own.at[self.half(q, wrap(p1 - 1), 0)], near.at[q, 2], down, 1),
            ]
        elif t == 1:
            plan = [(near.at[q, 0], near.at[q, 4], up, 2), (near.at[q, 1], near.at[q, 5], down, 2)]
        elif t == 2:
            plan = [
                (near.at[self.near_piece(q, wrap(p2 + k + 1))], self.far.at[q, k], (axis2, k + 1), 3)
                for k in range(3)
            ]
        elif t == 3:
            src = g.at[self.piece(q, p2)]
            plan = [(src, src, (axis2, k + 1), 4) for k in range(3)]
        elif t == 4:
            first, second = g.at[self.half(q, p1, 0)], g.at[self.half(q, p1, 1)]
            plan = [
                (first, first, up, 5), (second, second, down, 5),
                (second, second, up, 6), (first, first, down, 6),
            ]
        else:
            first = g.at[self.half(q, wrap(p1 - 1), 0)]
            second = g.at[self.half(q, wrap(p1 + 1), 1)]
            plan = [(first, first, up, 7), (second, second, down, 7)]
        return [
            pltpu.make_async_remote_copy(
                src_ref=src, dst_ref=dst, send_sem=self.sent, recv_sem=self.got.at[k],
                device_id=self.at(*target), device_id_type=MESH,
            )
            for src, dst, target, k in plan
        ]

    def wait(self, k):
        if k < 3:
            all_of = self.near.at[:, 2 * k : 2 * k + 2]
        elif k == 3:
            all_of = self.far
        else:
            all_of = self.g.at[self.row0 : self.row0 + (192 if k == 4 else 256)]
        pltpu.make_async_copy(all_of, all_of, self.got.at[k]).wait()

    def start(self, q, t):
        _, _, p1, p2 = self.ends(q)
        near, own = self.near, self.own
        if t == 1:
            near[q, 0] = near[q, 0] + own[self.half(q, wrap(p1 + 1), 0), :]
            near[q, 1] = near[q, 1] + own[self.half(q, wrap(p1 - 1), 1), :]
        elif t == 2:
            for h in range(2):
                total = near[q, 2 + h].astype(F32) + near[q, 4 + h].astype(F32)
                near[q, 2 + h] = (total + own[self.half(q, p1, h), :].astype(F32)).astype(BF16)
        elif t == 3:
            total = near[self.near_piece(q, p2)].astype(F32) + self.far[q, 0].astype(F32)
            total = total + (self.far[q, 1].astype(F32) + self.far[q, 2].astype(F32))
            self.g[self.piece(q, p2), :] = total.astype(BF16)
        for one in self.copies(q, t):
            one.start()

    def step(self, t):
        for k in ((), (0,), (1, 2), (3,), (4,), (5,), (6, 7))[t]:
            self.wait(k)
        if t < self.LAST:
            for q in range(2):
                self.start(q, t)

    def finish(self, ref):
        rows = 2 * (12 * 64 + 6 * 32) * self.own.shape[1] // WIDTH
        pltpu.make_async_copy(ref.at[0:rows], ref.at[0:rows], self.sent).wait()


def layers_kernel(
    lens_h, tok_h, cot_h, wqkv_h, wout_h, wup_h, wdown_h, gains_h, feats_h, cst_h,
    acts, in_grads, gsum, csum, esum, gain_out, feat_out,
    lens, xin, glow, aux, wqkv, wout, wup, wdown, gains, feats, cst, gbuf, cbuf, ebuf, near, near_c, near_e, far, far_c, far_e,
    fw, mask, rot, nrm, attn_in, mlp_in, tq, tk, pq, pk, qf, kf, vf, sb, den, att,
    mixed, hidden, ghp, gm, gproj, gpre, nx, inv_x,
    fpart, frx, fcs, fin, bpart, brx, bcs, bin_, xrx, small, srx, sall,
    load_s, frx_s, fin_s, facts_s, brx_s, bin_s, bout_s, x_s, xsib_s, ret_s, small_s,
    sent_s, got_s, all_s, give_s, give_back_s,
):
    s = lax.axis_index("section")
    t = lax.axis_index("tensor")
    dp = lax.axis_index("dp")
    zh = t // 2
    c = lax.rem(t, 2)
    sibling = {"tensor": zh * 2 + 1 - c}
    partner = {"tensor": lax.rem(t + 2, 4)}
    across = [{"section": 1 - s, "tensor": z * 2 + c} for z in range(2)]
    place = {"x": dp // 4, "y": lax.rem(dp, 4)}

    def at(axis, d):
        there = dict(place)
        there[axis] = lax.rem(place[axis] + d + 4, 4)
        return {"dp": there["x"] * 4 + there["y"]}

    def load(src, dst, k):
        return pltpu.make_async_copy(src, dst, load_s.at[k])

    first, second = slice(0, ROWS), slice(ROWS, ALL_ROWS)
    load_lens = load(lens_h, lens, 12)
    load_gains = load(gains_h, gains, 0)
    load_feats = load(feats_h, feats, 1)
    load_cst = load(cst_h, cst, 2)
    load_qkv = [load(wqkv_h.at[k], wqkv.at[k], 3 + k) for k in range(3)]
    load_up = load(wup_h, wup, 6)
    load_out = load(wout_h, wout, 7)
    load_down = load(wdown_h, wdown, 8)

    @pl.when(s == 0)
    def _():
        load(tok_h.at[first], xin.at[first], 9).start()
        for one in (load_gains, load_lens, load_feats, load_cst, *load_qkv):
            one.start()

    @pl.when(s == 1)
    def _():
        load(cot_h, glow, 9).start()
        for one in (load_down, load_out, load_lens, load_cst, load_gains, load_feats, *load_qkv, load_up):
            one.start()
        load(tok_h, aux, 11).start()

    barrier = pltpu.get_barrier_semaphore()
    peers = [sibling, partner, *across] + [at(axis, d) for axis in ("x", "y") for d in (1, 2, 3)]
    for target in peers:
        pl.semaphore_signal(barrier, inc=1, device_id=target, device_id_type=MESH)

    def remote(src, dst, sems, index, target):
        return pltpu.make_async_remote_copy(
            src_ref=src, dst_ref=dst, send_sem=sems.at[(0, *index)],
            recv_sem=sems.at[(1, *index)], device_id=target, device_id_type=MESH,
        )

    def micro_rows(m):
        if isinstance(m, int):
            return slice(m * ROWS, (m + 1) * ROWS)
        return pl.ds(pl.multiple_of(m * ROWS, ROWS), ROWS)

    def half_rows(m):
        return pl.ds(pl.multiple_of(m * ROWS + c * HALF, HALF), HALF)

    def part_rows(m, core, k):
        return pl.ds(pl.multiple_of(m * ROWS + core * HALF + k * 64, 64), 64)

    keep_rows = pl.ds(pl.multiple_of(c * HALF, HALF), HALF)
    give_rows = pl.ds(pl.multiple_of((1 - c) * HALF, HALF), HALF)

    def cols(n):
        return slice(n * 256, (n + 1) * 256)

    def f_swap(m):
        return remote(fpart.at[m, give_rows], frx.at[m], frx_s, (m,), sibling)

    def f_spread(m):
        return remote(fcs.at[m], fin.at[m], fin_s, (m,), partner)

    def f_share(m):
        return remote(acts.at[half_rows(m)], acts.at[half_rows(m)], facts_s, (m,), sibling)

    def b_swap(m):
        return remote(bpart.at[m, give_rows], brx.at[m], brx_s, (m,), sibling)

    def b_spread(m):
        return remote(bcs.at[m], bin_.at[m], bin_s, (m,), partner)

    def b_share(m):
        return remote(in_grads.at[half_rows(m)], in_grads.at[half_rows(m)], bout_s, (m,), sibling)

    def cross(src, m, z, k, arrival=False):
        here = z if arrival else zh
        rows = slice(k * 64, (k + 1) * 64)
        return pltpu.make_async_remote_copy(
            src_ref=src.at[m, rows], dst_ref=xrx.at[m, here, rows], send_sem=x_s.at[0, m, z, k],
            recv_sem=x_s.at[1, m, here, k], device_id=across[z], device_id_type=MESH,
        )

    def send_back(m, z, arrival=False):
        rows = part_rows(m, c, z if arrival else zh)
        return pltpu.make_async_remote_copy(
            src_ref=xin.at[rows], dst_ref=acts.at[rows], send_sem=ret_s.at[0, m, z],
            recv_sem=ret_s.at[1, m, z if arrival else zh], device_id=across[z], device_id_type=MESH,
        )

    def x_share(buf, m, k):
        rows = part_rows(m, c, k)
        return remote(buf.at[rows], buf.at[rows], xsib_s, (m, k), sibling)

    def chip_sum(part, rx, cs, m):
        cs[m] = (part[m, keep_rows].astype(F32) + rx[m].astype(F32)).astype(BF16)

    def send_across(cs, m):
        for k in range(2):
            for z in range(2):
                cross(cs, m, z, k).start()

    def arrived(src, m, k):
        for z in range(2):
            cross(src, m, z, k, arrival=True).wait_recv()
        rows = slice(k * 64, (k + 1) * 64)
        return xrx[m, 0, rows].astype(F32) + xrx[m, 1, rows].astype(F32)

    def context(m):
        length = lens[pl.ds(m, 1), :]
        first_end = length[:, 0:1]
        second_end = first_end + length[:, 1:2]
        third_end = second_end + length[:, 2:3]
        i = lax.broadcasted_iota(jnp.int32, (ROWS, ROWS), 0)
        j = lax.broadcasted_iota(jnp.int32, (ROWS, ROWS), 1)
        start = jnp.where(i >= first_end, first_end, 0)
        start = jnp.where(i >= second_end, second_end, start)
        start = jnp.where(i >= third_end, third_end, start)
        mask[m] = ((j <= i) & (j >= start)).astype(F32)
        hot = ((i - start) == j).astype(F32).astype(BF16)
        cosine = dot_nn(hot, cst[0:256, :]) + dot_nn(hot, cst[256:512, :])
        sine = dot_nn(hot, cst[512:768, :]) + dot_nn(hot, cst[768:1024, :])
        column = lax.rem(j, DIM)
        rot[m, 0] = cosine
        rot[m, 1] = jnp.where(column < ROT // 2, -sine, 0.0)
        rot[m, 2] = jnp.where(column >= ROT // 2, sine, 0.0)

    def norm_rows(rows):
        normed, _ = ln_rows(xin[rows, :].astype(F32))
        nrm[rows, :] = normed
        attn_in[rows, :] = (normed * gains[0:1, :]).astype(BF16)
        mlp_in[rows, :] = (normed * gains[1:2, :]).astype(BF16)

    def features(projected, m, turned_ref, phi_ref, low_ref):
        turned = (
            projected * rot[m, 0]
            + pltpu.roll(projected, LOCAL - ROT // 2, 1) * rot[m, 1]
            + pltpu.roll(projected, ROT // 2, 1) * rot[m, 2]
        )
        turned_ref[m] = turned
        high, rest = low_pieces(turned)
        square_high, square_rest = low_pieces(turned * turned)
        pieces = jnp.concatenate([high, rest, high, square_high, square_rest], axis=1)
        phi = fw[...] * jnp.exp(dot_nn(pieces, cst[1024:2304, :]))
        phi_ref[m] = phi
        low_ref[m] = phi.astype(BF16)

    def head_row(h):
        return cst[2816 + h * DIM : 2817 + h * DIM, :]

    def attend(m, up):
        queries, keys, values = qf[m], kf[m], vf[m]
        kept = mask[m] > 0.5
        total = jnp.zeros((ROWS, 2 * LOCAL), F32)
        for h in range(HEADS):
            row = head_row(h)
            scores = jnp.where(kept, dot_nt(queries * row, keys), 0.0).astype(BF16)
            sb[m, h] = scores
            right = jnp.concatenate(
                [values * row, jnp.broadcast_to(row, (ROWS, LOCAL))], axis=1
            )
            total = total + dot_nn(scores, right)
            if h % 2 == 0:
                up(2 + h // 2)
        norm = total[:, LOCAL:]
        attended = total[:, :LOCAL] / norm
        den[m] = norm
        att[m] = attended
        mixed[micro_rows(m), :] = attended.astype(BF16)

    def front(m):
        rows = micro_rows(m)
        normed_low = attn_in[rows, :]

        def up(n):
            pre = dot_nn(mlp_in[rows, :], wup[:, cols(n)])
            cdf, slope = normal_cdf(pre)
            hidden[rows, cols(n)] = (pre * cdf).astype(BF16)
            gpre[rows, cols(n)] = (ghp[rows, cols(n)] * slope).astype(BF16)
            ghp[rows, cols(n)] = slope

        queries = dot_nn(normed_low, wqkv[0])
        keys = dot_nn(normed_low, wqkv[1])
        up(0)
        features(queries, m, tq, pq, qf)
        up(1)
        features(keys, m, tk, pk, kf)
        vf[m] = dot_nn(normed_low, wqkv[2]).astype(BF16)
        attend(m, up)

    def back_out(m):
        rows = micro_rows(m)
        for n in range(4):
            tile = dot_nn(mixed[rows, :], wout[:, cols(n)])
            tile = tile + dot_nn(hidden[rows, :], wdown[:, cols(n)])
            fpart[m, :, cols(n)] = tile.astype(BF16)

    def grad_hidden(m, known):
        rows = micro_rows(m)
        for n in range(4):
            grad = dot_nt(glow[rows, :], wdown[cols(n), :])
            if known:
                gpre[rows, cols(n)] = (grad * ghp[rows, cols(n)]).astype(BF16)
            else:
                ghp[rows, cols(n)] = grad

    def grad_mixed(m):
        rows = micro_rows(m)
        gm[rows, :] = dot_nt(glow[rows, :], wout[...]).astype(BF16)

    def feature_back(grad_phi, m, turned_ref, phi_ref):
        grad_s = grad_phi * phi_ref[m]
        small[0, 2:3, 0:LOCAL] = small[0, 2:3, 0:LOCAL] + jnp.sum(grad_s, axis=0, keepdims=True)
        low = grad_s.astype(BF16)
        grad = dot_nn(low, cst[2304:2560, :]) - turned_ref[m] * dot_nn(low, cst[2560:2816, :])
        return (
            grad * rot[m, 0]
            - pltpu.roll(grad, LOCAL - ROT // 2, 1) * rot[m, 1]
            - pltpu.roll(grad, ROT // 2, 1) * rot[m, 2]
        )

    def attend_back(m):
        rows = micro_rows(m)
        grad_num = gm[rows, :].astype(F32) / den[m]
        grad_low = grad_num.astype(BF16)
        high, rest = low_pieces(grad_low.astype(F32) * att[m])
        ones = cst[2816:3072, :]
        grad_den = -(dot_nn(high, ones) + dot_nn(rest, ones))
        kept = mask[m] > 0.5
        queries, keys, values = qf[m], kf[m], vf[m]
        grad_q = jnp.zeros((ROWS, LOCAL), F32)
        grad_k = jnp.zeros((ROWS, LOCAL), F32)
        grad_v = jnp.zeros((ROWS, LOCAL), F32)
        for h in range(HEADS):
            row = head_row(h)
            given = grad_low * row
            grad_scores = dot_nt(given, values) + grad_den[:, h * DIM : h * DIM + 1]
            grad_scores = jnp.where(kept, grad_scores, 0.0).astype(BF16)
            grad_q = grad_q + dot_nn(grad_scores, keys * row)
            grad_k = grad_k + dot_tn(grad_scores, queries * row)
            grad_v = grad_v + dot_tn(sb[m, h], given)
            here = cols(h)
            grad_m = dot_nt(gpre[rows, :], wup[here, :])
            ghp[rows, here] = gains[1:2, here] * grad_m
            line = jnp.sum(nrm[rows, here] * grad_m, axis=0, keepdims=True)
            small[0, 1:2, here] = small[0, 1:2, here] + line
        gproj[0, rows, :] = feature_back(grad_q, m, tq, pq).astype(BF16)
        gproj[1, rows, :] = feature_back(grad_k, m, tk, pk).astype(BF16)
        gproj[2, rows, :] = grad_v.astype(BF16)

    def back_in(m):
        rows = micro_rows(m)
        for n in range(4):
            here = cols(n)
            grad_a = dot_nt(gproj[0, rows, :], wqkv[0, here, :])
            grad_a = grad_a + dot_nt(gproj[1, rows, :], wqkv[1, here, :])
            grad_a = grad_a + dot_nt(gproj[2, rows, :], wqkv[2, here, :])
            bpart[m, :, here] = (gains[0:1, here] * grad_a + ghp[rows, here]).astype(BF16)
            line = jnp.sum(nrm[rows, here] * grad_a, axis=0, keepdims=True)
            small[0, 0:1, here] = small[0, 0:1, here] + line

    def grads_down(n):
        gbuf[cols(n), :] = dot_tn(hidden[:, cols(n)], glow[...]).astype(BF16)
        if n % 2 == 1:
            sums[DOWN].start(n // 2, 0)

    def grads_up(n):
        rows = slice(1024 + n * 256, 1280 + n * 256)
        gbuf[rows, :] = dot_tn(mlp_in[:, cols(n)], gpre[...]).astype(BF16)
        if n % 2 == 1:
            sums[UP].start(n // 2, 0)

    def grads_attn(n):
        for k in range(3):
            cbuf[cols(n), cols(k)] = dot_tn(attn_in[:, cols(n)], gproj[k]).astype(BF16)
        if n % 2 == 1:
            sums[ATTN].start(n // 2, 0)

    def grads_out():
        for z in range(2):
            part = dot_tn(mixed[...], glow[:, z * 512 : (z + 1) * 512])
            ebuf[512 + z * 256 : 768 + z * 256, :] = part.astype(BF16)

    def finish_forward(m):
        f_spread(m).wait_recv()
        total = fcs[m].astype(F32) + fin[m].astype(F32)
        acts[half_rows(m), :] = (xin[half_rows(m), :].astype(F32) + total).astype(BF16)
        f_share(m).start()

    def finish_backward(m):
        b_spread(m).wait_recv()
        total = bcs[m].astype(F32) + bin_[m].astype(F32)
        normed, inv = ln_rows(xin[half_rows(m), :].astype(F32))
        in_grads[half_rows(m), :] = glow[half_rows(m), :].astype(F32) + ln_back(total, normed, inv)
        b_share(m).start()

    sums = [
        Sums(own, total, row0, *scratch, sent_s.at[j], got_s.at[j], place, at)
        for j, (own, total, row0, scratch) in enumerate(
            (
                (gbuf, gsum, 0, (near.at[0], far.at[0])),
                (gbuf, gsum, 1024, (near.at[1], far.at[1])),
                (cbuf, csum, 0, (near_c, far_c)),
                (ebuf, esum, 0, (near_e, far_e)),
            )
        )
    ]

    def give(z, arrival=False):
        place_there = z if arrival else zh
        return pltpu.make_async_remote_copy(
            src_ref=ebuf.at[512 + z * 256 : 768 + z * 256],
            dst_ref=ebuf.at[pl.ds(pl.multiple_of(place_there * 256, 256), 256)],
            send_sem=give_s.at[0, z], recv_sem=give_s.at[1, place_there],
            device_id=across[z], device_id_type=MESH,
        )

    def give_back(z, arrival=False):
        place_there = z if arrival else zh
        return pltpu.make_async_remote_copy(
            src_ref=esum.at[z * 256 : (z + 1) * 256],
            dst_ref=esum.at[pl.ds(pl.multiple_of(512 + place_there * 256, 256), 256)],
            send_sem=give_back_s.at[0, z], recv_sem=give_back_s.at[1, place_there],
            device_id=across[z], device_id_type=MESH,
        )

    def hop(j, step):
        sums[j].step(step)

    def small_step(k):
        def copy(k):
            if k < 2:
                return [remote(small.at[k], srx.at[k], small_s, (k,), (sibling, partner)[k])]
            axis = "xy"[k - 2]
            return [
                pltpu.make_async_remote_copy(
                    src_ref=small.at[k], dst_ref=sall.at[k - 2, place[axis]],
                    send_sem=all_s.at[0, k - 2], recv_sem=all_s.at[1, k - 2],
                    device_id=at(axis, d), device_id_type=MESH,
                )
                for d in (1, 2, 3)
            ]

        if k == -1:
            for j in range(2):
                copy(j)[0].wait_send()
                three = sall.at[j, 0:3]
                pltpu.make_async_copy(three, three, all_s.at[0, j]).wait()
            return
        if k in (1, 2):
            copy(k - 1)[0].wait_recv()
        if k > 2:
            three = sall.at[k - 3, 0:3]
            pltpu.make_async_copy(three, three, all_s.at[1, k - 3]).wait()
        if k in (1, 2):
            line = lax.broadcasted_iota(jnp.int32, (8, WIDTH), 0)
            small[k] = small[k - 1] + jnp.where(line < 2, srx[k - 1], 0.0)
        if k in (3, 4):
            parts = sall[k - 3]
            small[k] = (parts[0] + parts[1]) + (parts[2] + parts[3])
        if k in (2, 3):
            sall[k - 2, place["xy"[k - 2]]] = small[k]
        if k < 4:
            for one in copy(k):
                one.start()

    def spread_feats():
        exact = dot_exact(feats[...], cst[3072:3136, :].astype(F32), 0)
        fw[...] = jnp.sum(exact * heads_of(), axis=0, keepdims=True)

    def heads_of():
        return jnp.concatenate([head_row(h) for h in range(HEADS)], axis=0).astype(F32)

    def wait_all(*copies):
        for one in copies:
            one.wait()

    small[...] = jnp.zeros(small.shape, F32)

    @pl.when(s == 0)
    def _():
        def forward(m, carry):
            @pl.when(m == 0)
            def _():
                wait_all(load(tok_h.at[first], xin.at[first], 9), load_gains)
                for one in (load_up, load_out, load_down, load(tok_h.at[second], xin.at[second], 10)):
                    one.start()
                load(cot_h, aux, 11).start()

            for k in range(4):
                norm_rows(pl.ds(pl.multiple_of(m * ROWS + k * 64, 64), 64))

            @pl.when(m == 0)
            def _():
                wait_all(load_lens, load_feats, load_cst)
                spread_feats()

            context(m)

            @pl.when(m == 0)
            def _():
                wait_all(*load_qkv, load_up)

            front(m)

            @pl.when(m == 0)
            def _():
                wait_all(load_out, load_down)

            back_out(m)

            @pl.when(m == 0)
            def _():
                pl.semaphore_wait(barrier, len(peers))

            f_swap(m).start()

            @pl.when(m == 0)
            def _():
                wait_all(load(tok_h.at[second], xin.at[second], 10), load(cot_h, aux, 11))

            f_swap(m).wait_recv()
            chip_sum(fpart, frx, fcs, m)
            send_across(fcs, m)
            return carry

        lax.fori_loop(0, MICROS, forward, 0)

        def gradient_in(m):
            for z in range(2):
                send_back(m, z, arrival=True).wait_recv()
            normed, inv = ln_rows(acts[half_rows(m), :].astype(F32))
            nx[m] = normed
            inv_x[m] = jnp.broadcast_to(inv, (HALF, 128))
            f_share(m).start()
            for k in range(2):
                total = arrived(bcs, m, k)
                rows = slice(k * 64, (k + 1) * 64)
                back = ln_back(total, nx[m, rows], inv_x[m, rows, 0:1])
                grad = aux[part_rows(m, c, k), :].astype(F32) + back
                glow[part_rows(m, c, k), :] = grad.astype(BF16)
                x_share(glow, m, k).start()
            for k in range(2):
                x_share(glow, m, k).wait_recv()

        def backward(m, carry):
            last = m == MICROS - 1
            gradient_in(m)

            @pl.when(last)
            def _():
                for n in range(4):
                    grads_down(n)
                grads_out()
                for z in range(2):
                    give(z).start()

            grad_hidden(m, True)

            @pl.when(last)
            def _():
                for n in range(4):
                    grads_up(n)

            grad_mixed(m)
            attend_back(m)

            @pl.when(last)
            def _():
                hop(0, 1)
                for n in range(4):
                    grads_attn(n)

            back_in(m)
            b_swap(m).start()
            return carry

        lax.fori_loop(0, MICROS, backward, 0)
        hop(1, 1)
        for m in range(MICROS):
            for k in range(2):
                x_share(glow, m, k).wait_send()
                for z in range(2):
                    cross(fcs, m, z, k).wait_send()

    @pl.when(s == 1)
    def _():
        wait_all(load(cot_h, glow, 9), load_down)
        for m in range(MICROS):
            grad_hidden(m, False)
        wait_all(load_out, load_lens, load_cst, load_gains, load_feats)
        spread_feats()
        for m in range(MICROS):
            grad_mixed(m)
            context(m)
        wait_all(*load_qkv, load_up, load(tok_h, aux, 11))
        pl.semaphore_wait(barrier, len(peers))

        def cross_over(m):
            b_swap(m).wait_recv()
            chip_sum(bpart, brx, bcs, m)
            send_across(bcs, m)

        def take_in(m, k):
            total = arrived(fcs, m, k)
            own = part_rows(m, c, k)
            xin[own, :] = (aux[own, :].astype(F32) + total).astype(BF16)
            x_share(xin, m, k).start()

        def both(m, carry):
            @pl.when(m == 0)
            def _():
                for k in range(2):
                    take_in(0, k)
                    norm_rows(part_rows(0, c, k))
                for z in range(2):
                    send_back(0, z).start()

            @pl.when(m == 1)
            def _():
                for k in range(2):
                    norm_rows(part_rows(1, c, k))

            for k in range(2):
                x_share(xin, m, k).wait_recv()
                norm_rows(part_rows(m, 1 - c, k))

            @pl.when(m == 1)
            def _():
                cross_over(0)

            front(m)
            attend_back(m)

            @pl.when(m == 0)
            def _():
                for k in range(2):
                    take_in(1, k)
                for z in range(2):
                    send_back(1, z).start()

            back_in(m)
            b_swap(m).start()
            return carry

        lax.fori_loop(0, MICROS, both, 0)
        grads_down(0)
        grads_down(1)
        cross_over(1)
        grads_down(2)
        grads_down(3)
        for n in range(4):
            grads_up(n)
        hop(0, 1)
        for n in range(4):
            grads_attn(n)
        grads_out()
        for m in range(MICROS):
            back_out(m)
            f_swap(m).start()
        hop(1, 1)
        for m in range(MICROS):
            for z in range(2):
                for k in range(2):
                    cross(bcs, m, z, k).wait_send()
        for m in range(MICROS):
            for k in range(2):
                x_share(xin, m, k).wait_send()
                send_back(m, k).wait_send()

    small_step(0)
    for part, step in ORDER:
        if part == OUT:

            @pl.when(s == 1)
            def _():
                if step == 0:
                    for z in range(2):
                        give(z, arrival=True).wait_recv()
                    for q in range(2):
                        sums[OUT].start(q, 0)
                else:
                    hop(OUT, step)
                if step == Sums.LAST:
                    for z in range(2):
                        give_back(z).start()

            continue
        if (part, step) == (DOWN, 3):

            @pl.when(s == 0)
            def _():
                for m in range(MICROS):
                    b_swap(m).wait_recv()
                    chip_sum(bpart, brx, bcs, m)

            @pl.when(s == 1)
            def _():
                for m in range(MICROS):
                    f_swap(m).wait_recv()
                    chip_sum(fpart, frx, fcs, m)
                    f_spread(m).start()

            for m in range(MICROS):
                b_spread(m).start()

        if part == DOWN and 2 < step < 6:
            small_step(step - 2)
        hop(part, step)
        if part != ATTN:
            continue
        if step == 4:
            for m in range(MICROS):
                finish_backward(m)

            @pl.when(s == 1)
            def _():
                for m in range(MICROS):
                    finish_forward(m)
                    f_spread(m).wait_send()

        if step == 5:
            small_step(4)
            gain_out[...] = small[4, 0:2, :]
            line = jnp.broadcast_to(small[4, 2:3, 0:LOCAL] / fw[...], (HEADS, LOCAL))
            feat_out[...] = dot_exact(line * heads_of(), cst[3072:3136, :].astype(F32), 1)
            small_step(-1)
            for m in range(MICROS):
                f_share(m).wait_recv()
                b_share(m).wait_recv()
                for one in (f_swap(m), f_share(m), b_swap(m), b_spread(m), b_share(m)):
                    one.wait_send()
    for one in sums[:OUT]:
        one.finish(gbuf)

    @pl.when(s == 0)
    def _():
        for z in range(2):
            give(z).wait_send()
            give_back(z, arrival=True).wait_recv()

    @pl.when(s == 1)
    def _():
        sums[OUT].finish(gbuf)
        for z in range(2):
            give_back(z).wait_send()


def layers(lengths, tok, cot, wqkv, wout, wup, wdown, gains, feats):
    vm = pl.BlockSpec(memory_space=pltpu.VMEM)
    far_off = pl.BlockSpec(memory_space=pl.ANY)

    def low(*shape):
        return pltpu.VMEM(shape, BF16)

    def wide(*shape):
        return pltpu.VMEM(shape, F32)

    full = (MICROS, ROWS, WIDTH)
    half = (MICROS, HALF, WIDTH)
    square = (MICROS, ROWS, LOCAL)
    rows = (ALL_ROWS, WIDTH)
    sems = pltpu.SemaphoreType.DMA
    return pl.pallas_call(
        layers_kernel,
        out_shape=(
            low(*rows), wide(*rows), low(2 * WIDTH, WIDTH), low(WIDTH, 768), low(WIDTH, 512),
            wide(2, WIDTH), wide(HEADS, DIM),
        ),
        in_specs=[far_off] * 10,
        out_specs=(vm,) * 7,
        scratch_shapes=[
            pltpu.VMEM((MICROS, 4), jnp.int32), low(*rows), low(*rows), low(*rows),
            low(3, WIDTH, LOCAL), low(LOCAL, WIDTH), low(WIDTH, WIDTH), low(WIDTH, WIDTH),
            wide(2, WIDTH), wide(HEADS, DIM), low(3136, LOCAL),
            low(2 * WIDTH, WIDTH), low(WIDTH, 768), low(WIDTH, 512),
            low(2, 2, 6, 64, WIDTH), low(2, 6, 64, 768), low(2, 6, 64, 512),
            low(2, 2, 3, 32, WIDTH), low(2, 3, 32, 768), low(2, 3, 32, 512),
            wide(1, LOCAL), wide(*square), wide(MICROS, 3, ROWS, LOCAL),
            wide(*rows), low(*rows), low(*rows),
            wide(*square), wide(*square), wide(*square), wide(*square),
            low(*square), low(*square), low(*square),
            low(MICROS, HEADS, ROWS, ROWS), wide(*square), wide(*square),
            low(ALL_ROWS, LOCAL), low(*rows), wide(*rows), low(ALL_ROWS, LOCAL),
            low(3, ALL_ROWS, LOCAL), low(*rows), wide(*half), wide(MICROS, HALF, 128),
            low(*full), low(*half), low(*half), low(*half),
            low(*full), low(*half), low(*half), low(*half),
            low(MICROS, 2, HALF, WIDTH), wide(5, 8, WIDTH), wide(2, 8, WIDTH), wide(2, 4, 8, WIDTH),
            sems((13,)),
            sems((2, MICROS)), sems((2, MICROS)), sems((2, MICROS)),
            sems((2, MICROS)), sems((2, MICROS)), sems((2, MICROS)),
            sems((2, MICROS, 2, 2)), sems((2, MICROS, 2)), sems((2, MICROS, 2)), sems((2, 2)),
            sems((4,)), sems((4, 8)), sems((2, 2)), sems((2, 2)), sems((2, 2)),
        ],
        compiler_params=pltpu.CompilerParams(
            collective_id=0, has_side_effects=True, vmem_limit_bytes=53 * 2**20
        ),
        name="layers",
    )(lengths, tok, cot, wqkv, wout, wup, wdown, gains, feats, jnp.asarray(constants()))


def widen_kernel(
    grads, attn, out_part, acts, in_grads, gains, feats, o_down, o_up, o_qkv, o_out, o_acts, o_in, o_gains, o_feats,
    down, up, qkv, out, sems, more,
):
    def copies(n):
        rows = pl.ds(pl.multiple_of(n * 256, 256), 256)
        tall = pl.ds(pl.multiple_of(lax.rem(n, 2) * 128, 128), 128)
        broad = pl.ds(pl.multiple_of(n // 2 * 512, 512), 512)
        return [
            pltpu.make_async_copy(down.at[rows], o_down.at[rows], sems.at[0, n]),
            pltpu.make_async_copy(up.at[rows], o_up.at[rows], sems.at[1, n]),
            pltpu.make_async_copy(qkv.at[:, rows], o_qkv.at[:, rows], sems.at[2, n]),
            pltpu.make_async_copy(out.at[n], o_out.at[tall, broad], sems.at[3, n]),
        ]

    whole = [
        pltpu.make_async_copy(src, dst, more.at[k])
        for k, (src, dst) in enumerate(
            ((in_grads, o_in), (acts, o_acts), (gains, o_gains), (feats, o_feats))
        )
    ]
    for one in whole:
        one.start()

    def body(n, carry):
        rows = pl.ds(pl.multiple_of(n * 256, 256), 256)
        first, second, third, fourth = copies(n)
        down[rows, :] = grads[rows, :].astype(F32)
        first.start()
        up[rows, :] = grads[pl.ds(pl.multiple_of(WIDTH + n * 256, 256), 256), :].astype(F32)
        second.start()
        for k in range(3):
            qkv[k, rows, :] = attn[rows, k * 256 : (k + 1) * 256].astype(F32)
        third.start()
        out[n] = out_part[pl.ds(pl.multiple_of(512 + n * 128, 128), 128), :].astype(F32)
        fourth.start()
        return carry

    lax.fori_loop(0, 4, body, 0)
    for n in range(4):
        for one in copies(n):
            one.wait()
    for one in whole:
        one.wait()


def widen(grads, attn, out_part, acts, in_grads, gains, feats):
    vm = pl.BlockSpec(memory_space=pltpu.VMEM)
    far_off = pl.BlockSpec(memory_space=pl.ANY)

    def like(*shape):
        return jax.ShapeDtypeStruct(shape, F32)

    def wide(*shape):
        return pltpu.VMEM(shape, F32)

    return pl.pallas_call(
        widen_kernel,
        in_specs=[vm] * 7,
        out_specs=[far_off] * 8,
        out_shape=(
            like(WIDTH, WIDTH), like(WIDTH, WIDTH), like(3, WIDTH, LOCAL), like(LOCAL, WIDTH),
            jax.ShapeDtypeStruct((ALL_ROWS, WIDTH), BF16), like(ALL_ROWS, WIDTH),
            like(2, WIDTH), like(HEADS, DIM),
        ),
        scratch_shapes=[
            wide(WIDTH, WIDTH), wide(WIDTH, WIDTH), wide(3, WIDTH, LOCAL), wide(4, 128, 512),
            pltpu.SemaphoreType.DMA((4, 4)), pltpu.SemaphoreType.DMA((4,)),
        ],
        compiler_params=pltpu.CompilerParams(vmem_limit_bytes=40 * 2**20),
        name="widen",
    )(grads, attn, out_part, acts, in_grads, gains, feats)


def per_device(
    tokens, lengths, cotangent, qkv_weight, out_weight, up_weight, down_weight, norm_gains,
    feat_weights,
):
    acts, in_grads, grads, attn, out_part, gains, feats = layers(
        lengths, tokens, cotangent, jnp.transpose(qkv_weight[0], (1, 0, 2)), out_weight[0],
        up_weight[0], down_weight[0], norm_gains[0], feat_weights[0],
    )
    down, up, qkv, out, acts, in_grads, gains, feats = widen(
        grads, attn, out_part, acts, in_grads, gains, feats
    )
    qkv = jnp.transpose(qkv, (1, 0, 2))
    return tuple(one[None] for one in (acts, in_grads, qkv, out, up, down, gains, feats))


PLACED = (
    P("dp", None),
    P("dp", None),
    P("dp", None),
    P("section", None, None, "tensor"),
    P("section", "tensor", None),
    P("section", None, "tensor"),
    P("section", "tensor", None),
    P("section", None, None),
    P("section", "tensor", None),
)
GIVEN = (
    P("section", "dp", None),
    P("section", "dp", None),
    P("section", None, None, "tensor"),
    P("section", "tensor", None),
    P("section", None, "tensor"),
    P("section", "tensor", None),
    P("section", None, None),
    P("section", "tensor", None),
)


def solution(mesh):
    return jax.shard_map(
        per_device, mesh=mesh, in_specs=PLACED, out_specs=GIVEN, check_vma=False
    )
```

profile of v0, /device:TPU:0, one launch (start us, length us, event | category | flops | bytes accessed | tf_op | source)
XLA Modules:
  0.0 120.9 jit_solution(12608521521711760254)
XLA Ops:
  0.6 114.4 %layers.1 = (bf16[512,1024]{1,0:T(8,128)(2,1)S(1)}, f32[512,1024]{1,0:T(8,128)S(1)}, bf16[2048,1024]{1,0:T(8,128)(2,1)S(1)}, bf16[1024,768]{1,0:T(8,128)(2,1)S(1...) custom-call(s32[2,4]{1,0:T(2,128)} %lens_h.1, bf16[512,1024]{1,0:T(8,128)(2,1)} %tok_h.1, ...), custom_call_target="tpu_custom_call" | custom-call | tf_op jit(solution)/shard_map/layers/pallas_call | solution.py:920
  115.1 5.7 %widen.1 = (f32[1024,1024]{1,0:T(8,128)}, f32[1024,1024]{1,0:T(8,128)}, f32[3,1024,256]{2,1,0:T(8,128)}, f32[256,1024]{1,0:T(8,128)}, bf16[512,1024]{1,0:T(8,128...) custom-call(bf16[2048,1024]{1,0:T(8,128)(2,1)S(1)} %get-tuple-element.23.grads, ...), custom_call_target="tpu_custom_call" | custom-call | tf_op jit(solution)/shard_map/widen/pallas_call | solution.py:1014
where the time goes:
time: 123 us; the launch traced here: 121 us
  Pallas kernels  120 us (98%)
    pallas_call x1, Pallas kernels, layers(): pl.pallas_call(layers_kernel, out_shape=(low(*rows), wide(*rows), low(2 *...  114 us
    pallas_call x1, Pallas kernels, widen(): pl.pallas_call(widen_kernel, in_specs=[vm] * 7, out_specs=[far_off] * 8,...  5.67 us

commit v1 on v0

--- a/solution.py
+++ b/solution.py
@@ -811,9 +811,6 @@
         for n in range(4):
             grads_attn(n)
         grads_out()
-        for m in range(MICROS):
-            back_out(m)
-            f_swap(m).start()
         hop(1, 1)
         for m in range(MICROS):
             for z in range(2):
@@ -831,6 +828,9 @@
             @pl.when(s == 1)
             def _():
                 if step == 0:
+                    for m in range(MICROS):
+                        back_out(m)
+                        f_swap(m).start()
                     for z in range(2):
                         give(z, arrival=True).wait_recv()
                     for q in range(2):
@@ -842,7 +842,7 @@
                         give_back(z).start()
 
             continue
-        if (part, step) == (DOWN, 3):
+        if (part, step) == (UP, 3):
 
             @pl.when(s == 0)
             def _():

time: 123 us -> 121 us (0.984); the launches traced: 121 us -> 121 us
  no operation moved by 1% of the time
where the time goes in v1:
time: 121 us
  Pallas kernels  120 us (99%)
    pallas_call x1, Pallas kernels, layers(): pl.pallas_call(layers_kernel, out_shape=(low(*rows), wide(*rows), low(2 *...  114 us
    pallas_call x1, Pallas kernels, widen(): pl.pallas_call(widen_kernel, in_specs=[vm] * 7, out_specs=[far_off] * 8,...  5.67 us

profile of v1, /device:TPU:0, one launch (start us, length us, event | category | flops | bytes accessed | tf_op | source)
XLA Modules:
  0.0 120.8 jit_solution(10074736134540929544)
XLA Ops:
  0.6 114.3 %layers.1 = (bf16[512,1024]{1,0:T(8,128)(2,1)S(1)}, f32[512,1024]{1,0:T(8,128)S(1)}, bf16[2048,1024]{1,0:T(8,128)(2,1)S(1)}, bf16[1024,768]{1,0:T(8,128)(2,1)S(1...) custom-call(s32[2,4]{1,0:T(2,128)} %lens_h.1, bf16[512,1024]{1,0:T(8,128)(2,1)} %tok_h.1, ...), custom_call_target="tpu_custom_call" | custom-call | tf_op jit(solution)/shard_map/layers/pallas_call | solution.py:920
  114.9 5.7 %widen.1 = (f32[1024,1024]{1,0:T(8,128)}, f32[1024,1024]{1,0:T(8,128)}, f32[3,1024,256]{2,1,0:T(8,128)}, f32[256,1024]{1,0:T(8,128)}, bf16[512,1024]{1,0:T(8,128...) custom-call(bf16[2048,1024]{1,0:T(8,128)(2,1)S(1)} %get-tuple-element.23.grads, ...), custom_call_target="tpu_custom_call" | custom-call | tf_op jit(solution)/shard_map/widen/pallas_call | solution.py:1014
